TPU v7x, 32 devices: a whole 2x2x4 slice. The times are simulated.
32 devices in a mesh: pb: 8 (over y, x, core), ga: 4 (over z).
Axes of the slice: x: 2, y: 2, z: 4, core: 2. Of those that a mesh axis runs over, the one named last changes fastest.
Arguments:
- elements: bfloat16 [8, 64, 112, 2048], P('pb', None, None, 'ga'), may hold values from -0.75 to 0.75
- screened: bfloat16 [8, 2048, 2048], P('pb', 'ga'), may hold values from -0.125 to 0.125
- counts: int32 [8], P('pb'), may hold values from 1536 to 2048
- k_minus_q: int32 [8], P('pb'), may hold values from 0 to 575
- occupation: float32 [576, 64], replicated, may hold values from 0.25 to 1
Outputs:
- sigma: float32 [112, 112], P('ga')
Inputs may be any that keep to these rules, and one draw needn't show every extreme that they name: k_minus_q[q] is a row of occupation.
All inputs are finite; a program needn't handle non-finite values.
Results may differ from a plain program's by a relative error of at most 0.0029.
Values may be sent and summed in bfloat16 or wider, within the bound.
A program may use at most 128 MiB of HBM per device.

v0:
```python
import jax
import jax.numpy as jnp
from jax import lax
from jax.sharding import PartitionSpec as P

NB = 32


def on_device(elements, screened, counts, k_minus_q, occupation):
    q_count, n_band, n_state, g_slab = elements.shape
    groups = lax.axis_size("ga")
    my_index = lax.axis_index("ga")
    g_total = g_slab * groups
    n_cycles = g_total // (groups * NB)
    rows_true = my_index * g_slab + jnp.arange(g_slab, dtype=jnp.int32)
    inside = (rows_true[None, :] < counts[:, None]).astype(jnp.bfloat16)
    masked = elements * inside[:, None, None, :]
    k_index = jnp.arange(occupation.shape[0], dtype=jnp.int32)
    weights = jnp.sum(
        jnp.where(
            k_index[None, :, None] == k_minus_q[:, None, None], occupation[None], jnp.float32(0.0)
        ),
        axis=1,
    )
    partial_value = jnp.zeros((n_state, n_state), jnp.float32)
    columns = lax.all_to_all(screened, "ga", split_axis=2, concat_axis=1, tiled=True)
    columns = (
        columns.reshape(q_count, groups, n_cycles, NB, g_slab)
        .transpose(0, 2, 1, 3, 4)
        .reshape(q_count, g_total, g_slab)
    )

    def accumulate(running, segment, offset, screen_q=columns[0]):
        piece_rows = segment.shape[2]
        return jnp.dot(
            segment.reshape(n_band * n_state, piece_rows),
            screen_q,
            preferred_element_type=jnp.float32,
        )

    start_sum = jnp.zeros((n_band * n_state, g_slab), jnp.float32)
    product = accumulate(
        start_sum, lax.all_gather(masked[0], "ga", axis=2, tiled=True), jnp.int32(0)
    )
    product = product.astype(jnp.bfloat16).reshape(n_band, n_state, g_slab)
    pair_terms = jnp.einsum("vmg,vng->vmn", product, masked[0], preferred_element_type=jnp.float32)
    partial_value = partial_value - jnp.einsum(
        "v,vmn->mn", weights[0], pair_terms, precision=lax.Precision.HIGHEST
    )
    row_share = lax.psum_scatter(partial_value, "ga", scatter_dimension=0, tiled=True)
    result_rows = lax.psum(row_share, "pb")
    return result_rows


def solution(mesh):
    return jax.shard_map(
        on_device,
        mesh=mesh,
        in_specs=(P("pb", None, None, "ga"), P("pb", "ga", None), P("pb"), P("pb"), P()),
        out_specs=P("ga", None),
        check_vma=False,
    )
```

profile of v0, /device:TPU:0, one launch (start us, length us, event | category | flops | bytes accessed | tf_op | source)
XLA Modules:
  0.0 628.6 jit_solution(8233131330537181441)
XLA Ops:
  6.5 0.0 all-gather.3.cloned.1.call-start
  7.2 6.5 %broadcast_multiply_fusion = bf16[1,64,112,512]{3,2,1,0:T(8,128)(2,1)} fusion(bf16[1,64,112,512]{3,2,1,0:T(8,128)(2,1)} %param.5, bf16[512]{0:T(512)(128)(2,1)S(1)} %fusion.5), kind=kLoop, calls=%fused_computation.5 | loop fusion | flops 3670016 | bytes 14681088 | tf_op jit(solution)/shard_map/mul | solution.py:17
  13.8 0.0 copy-start
  13.8 0.0 all-gather.3.cloned.1.call-update
  13.8 1.6 copy-done
  15.3 7.6 %copy.10 = bf16[1,512,2048]{1,0,2:T(2,128)(2,1)} copy(bf16[1,512,2048]{2,1,0:T(8,128)(2,1)S(1)} %copy-done) | data formatting | bytes 4194304 | tf_op args[1]
  22.9 0.5 broadcast.22
  23.4 0.0 copy-start.1
  23.4 14.2 %reduce.2 = bf16[2048,512]{1,0:T(8,128)(2,1)S(1)} reduce(bf16[2048,1,512]{2,1,0:T(2,128)(2,1)} %bitcast.31, bf16[]{:T(256)} %broadcast.22), dimensions={1}, to_apply=%bitcast.22.reduce_sub_computation | reduce | bytes 4194306
  37.7 2.8 reshape.45
  40.5 6.4 %all-to-all-start = ((bf16[4,2,131072]{2,1,0:T(2,128)(2,1)}), bf16[4,2,131072]{2,1,0:T(2,128)(2,1)S(1)}, u32[]{:S(2)}, u32[]{:S(2)}) async-start(bf16[4,2,131072]{2,1,0:T(2,128)(2,1)} %reshape.45), calls=%async_computation | async-start | bytes 4194304 | tf_op jit(solution)/shard_map/all_to_all | solution.py:26
  47.5 0.0 copy-done.1
  47.5 0.1 select_reduce_fusion
  47.6 96.3 %all-to-all-done = bf16[4,2,131072]{2,1,0:T(2,128)(2,1)S(1)} async-done(((bf16[4,2,131072]{2,1,0:T(2,128)(2,1)}), bf16[4,2,131072]{2,1,0:T(2,128)(2,1)S(1)}, u32[]{:S(2)}, u32[]{:S(2)}) %all-to-all-start) | async-done | bytes 2097184 | tf_op jit(solution)/shard_map/all_to_all | solution.py:26
  143.9 3.3 reshape.46
  147.3 2.9 copy.15
  150.2 2.4 copy.11
  152.5 3.3 copy.12
  155.8 398.8 %all-gather.3.cloned.1.call-done = bf16[1,64,112,2048]{3,2,1,0:T(8,128)(2,1)} async-done(((bf16[1,64,112,512]{3,2,1,0:T(8,128)(2,1)}), bf16[1,64,112,2048]{3,2,1,0:T(8,128)(2,1)}) %all-gather.3.cloned.1.call-update) | async-done | bytes 29360144 | tf_op jit(solution)/shard_map/all_gather | solution.py:43
  554.7 21.8 %convolution_convert_fusion = bf16[7168,512]{1,0:T(8,128)(2,1)} fusion(bf16[7168,2048]{1,0:T(8,128)(2,1)} %bitcast.38, bf16[2048,512]{1,0:T(8,128)(2,1)} %bitcast.36), kind=kOutput, calls=%fused_computation | convolution fusion | flops 15036055552 | bytes 38797312 | tf_op jit(solution)/shard_map/dot_general | solution.py:35
  576.5 0.0 slice-done
  576.5 0.0 slice-done.1
  576.5 0.0 copy-start.2
  576.5 5.2 fusion.1
  581.7 2.8 fusion.3
  584.5 11.3 %fusion = f32[32,112]{1,0:T(8,128)S(1)} fusion(f32[112,112]{1,0:T(8,128)S(1)} %broadcast_subtract_fusion), kind=kCustom, calls=%all-reduce-scatter | all-reduce-scatter fusion | flops 14337 | bytes 65024
  595.8 1.6 collective-permute-start
  597.4 0.0 copy-done.2
  597.4 0.6 dynamic-slice.4
  598.7 0.1 collective-permute-done
  598.8 0.1 concatenate
  598.9 22.9 %psum.7 = f32[28,112]{1,0:T(8,128)} all-reduce(f32[28,112]{1,0:T(8,128)S(1)} %constant_dynamic-slice_fusion), channel_id=1, replica_groups=mesh['pb'=8,'ga'=4] {'pb'}, use_global_device_ids=true, to_apply=%region_2.3 | all-reduce | flops 3136 | bytes 25088 | tf_op jit(solution)/shard_map/psum | solution.py:51
  (8 shorter events, 0.0 us)
Async XLA Ops:
  6.5 548.1 %all-gather.3.cloned.1.call-start = ((), (), s32[]{:S(2)}) async-start(), calls=%async_computation.1 | async-start | bytes 36700160 | tf_op jit(solution)/shard_map/all_gather | solution.py:43
  13.8 1.6 copy-start
  23.4 24.1 %copy-start.1 = (f32[576,64]{0,1:T(8,128)S(1)}, f32[576,64]{0,1:T(8,128)}, u32[]{:S(2)}) copy-start(f32[576,64]{0,1:T(8,128)} %param.9) | copy-start | bytes 442372
  40.5 103.5 %all-to-all-start = ((bf16[4,2,131072]{2,1,0:T(2,128)(2,1)}), bf16[4,2,131072]{2,1,0:T(2,128)(2,1)S(1)}, u32[]{:S(2)}, u32[]{:S(2)}) async-start(bf16[4,2,131072]{2,1,0:T(2,128)(2,1)} %reshape.45), calls=%async_computation | async-start | bytes 4194304 | tf_op jit(solution)/shard_map/all_to_all | solution.py:26
  152.5 424.0 %slice-start = ((s8[7340032]{0:T(1024)(128)(4,1)}), s8[3145728]{0:T(1024)(128)(4,1)S(1)}, s32[]{:S(2)}) async-start(s8[7340032]{0:T(1024)(128)(4,1)} %bitcast.29), calls=%async_computation.2 | async-start | bytes 6291456
  554.7 21.9 %slice-start.1 = ((s8[7340032]{0:T(1024)(128)(4,1)}), s8[4194304]{0:T(1024)(128)(4,1)S(1)}, s32[]{:S(2)}) async-start(s8[7340032]{0:T(1024)(128)(4,1)} %bitcast.29), calls=%async_computation.3 | async-start | bytes 8388608
  576.5 20.9 %copy-start.2 = (u32[32]{0:T(128)S(1)}, u32[32]{0:T(128)}, u32[]{:S(2)}) copy-start(u32[32]{0:T(128)} %constant.15) | copy-start | bytes 388
  595.8 3.0 collective-permute-start
Sparse Core Ops, SparseCore 0:
  13.9 540.7 all-gather.2
where the time goes:
time: 629 us
  waiting for transfers between devices  495 us (79%)
  blocking collectives  34.2 us (5%)
  matrix products  29.8 us (5%)
  local copies, waits for them, and re-layouts  25 us (4%)
  other arithmetic  20.9 us (3%)
  between operations  15.4 us (2%)
  starting transfers between devices  7.98 us (1%)
    all_gather x1, waiting for transfers between devices, on_device(): lax.all_gather(masked[0], 'ga', axis=2, tiled=True)  399 us
    all_to_all x1, waiting for transfers between devices, on_device(): lax.all_to_all(screened, 'ga', split_axis=2, concat_axis=1, tiled=True)  96.3 us
    psum x1, blocking collectives, on_device(): result_rows = lax.psum(row_share, 'pb')  22.9 us
    dot_general x1, matrix products, accumulate(): jnp.dot(segment.reshape(n_band * n_state, piece_rows), screen_q, preferre...  21.8 us
    unnamed x19, local copies, waits for them, and re-layouts  19.4 us
    unnamed x2, other arithmetic  14.2 us
  transfers between devices with their start and end apart: 3, of which 3 were waited for; matrix products, arithmetic and copies ran while one was open for 6% of the time, Pallas kernels for 0%

commit v1 on v0

v1 whole, which is shorter than its diff:
```python
import functools

import jax
import jax.numpy as jnp
from jax import lax
from jax.experimental import pallas as pl
from jax.experimental.pallas import tpu as pltpu
from jax.sharding import PartitionSpec as P

NB = 32
MESH = pl.DeviceIdType.MESH


def kernel(
    n, n_pb, vg, wc,
    elements, screened, counts, k_minus_q, occupation, out,
    mbuf, wbuf, wown, occ, pair, acc, parts, ga_in, pb_in,
    local_sem, wsend, wrecv, msend, mrecv, gsend, grecv, psend, precv,
):
    me = lax.axis_index("ga")
    my_pb = lax.axis_index("pb")
    _, v_per, n_state, g_slab = elements.shape
    n_cycles, _, g_total = screened.shape
    rows = n_state // n
    nk = v_per // vg
    nc = n_cycles // wc

    def peer(offset):
        return lax.rem(me + offset, n)

    def pb_peer(offset):
        return lax.rem(my_pb + offset, n_pb)

    my_lanes = pl.ds(pl.multiple_of(me * g_slab, g_slab), g_slab)
    own_w = pltpu.make_async_copy(screened, wown, local_sem.at[0])
    own_m = pltpu.make_async_copy(elements.at[me], mbuf.at[:, :, my_lanes], local_sem.at[1])
    own_occ = pltpu.make_async_copy(occupation, occ, local_sem.at[2])
    own_w.start()
    own_m.start()
    own_occ.start()

    barrier = pltpu.get_barrier_semaphore()
    for offset in range(1, n):
        pl.semaphore_signal(barrier, inc=1, device_id={"ga": peer(offset)}, device_id_type=MESH)
    for offset in range(1, n_pb):
        pl.semaphore_signal(barrier, inc=1, device_id={"pb": pb_peer(offset)}, device_id_type=MESH)
    pl.semaphore_wait(barrier, n - 1 + n_pb - 1)

    def m_copy(k, offset):
        return pltpu.make_async_remote_copy(
            src_ref=elements.at[peer(offset), pl.ds(k * vg, vg)],
            dst_ref=mbuf.at[pl.ds(k * vg, vg), :, my_lanes],
            send_sem=msend.at[offset - 1, k],
            recv_sem=mrecv.at[offset - 1, k],
            device_id={"ga": peer(offset)},
            device_id_type=MESH,
        )

    def w_copy(source, chunk, step):
        side = 0 if step < 0 else 1
        return pltpu.make_async_remote_copy(
            src_ref=wbuf.at[pl.ds(chunk * wc, wc), source],
            dst_ref=wbuf.at[pl.ds(chunk * wc, wc), source],
            send_sem=wsend.at[side, source, chunk],
            recv_sem=wrecv.at[source, chunk],
            device_id={"ga": lax.rem(me + step + n, n)},
            device_id_type=MESH,
        )

    started = []

    def send_next_m():
        if len(started) < nk:
            for offset in range(n - 1, 0, -1):
                m_copy(len(started), offset).start()
            started.append(0)

    own_w.wait()
    count = counts[0]
    column = lax.broadcasted_iota(jnp.int32, (NB, g_total), 1)
    row = lax.broadcasted_iota(jnp.int32, (NB, g_total), 0)

    for chunk in range(nc):

        def mask_block(c, carry):
            g = row + (c * n + me) * NB
            inside = jnp.logical_and(g < count, column < count)
            block = wown[c].astype(jnp.float32)
            wbuf[c, me] = jnp.where(inside, block, 0.0).astype(jnp.bfloat16)
            return carry

        lax.fori_loop(chunk * wc, (chunk + 1) * wc, mask_block, 0)

        @pl.when(me > 0)
        def _():
            w_copy(me, chunk, -1).start()

        @pl.when(me < n - 1)
        def _():
            w_copy(me, chunk, 1).start()

        if chunk == 0:
            send_next_m()

    for distance in range(1, n):
        for chunk in range(nc):
            source = me - distance

            @pl.when(source >= 0)
            def _():
                w_copy(source, chunk, 1).wait_recv()

                @pl.when(me < n - 1)
                def _():
                    w_copy(source, chunk, 1).start()

            source_up = me + distance

            @pl.when(source_up < n)
            def _():
                w_copy(source_up, chunk, -1).wait_recv()

                @pl.when(me > 0)
                def _():
                    w_copy(source_up, chunk, -1).start()

            send_next_m()
    while len(started) < nk:
        send_next_m()

    own_m.wait()
    own_occ.wait()
    weights = occ[pl.ds(k_minus_q[0], 1), :]
    band = lax.broadcasted_iota(jnp.int32, weights.shape, 1)
    acc[...] = jnp.zeros_like(acc)
    ht = min(512, g_total)

    def group(k, carry):
        for offset in range(1, n):
            m_copy(k, offset).wait_recv()
        pair[...] = jnp.zeros_like(pair)

        def tile(h, inner):
            lanes = pl.ds(pl.multiple_of(h * ht, ht), ht)
            left = mbuf[pl.ds(k * vg, vg)].reshape(vg * n_state, g_total)
            w = wbuf[:, :, :, lanes].reshape(g_total, ht)
            product = jnp.dot(left, w, preferred_element_type=jnp.float32).astype(jnp.bfloat16)
            for v in range(vg):
                pair[v] += lax.dot_general(
                    product[v * n_state : (v + 1) * n_state],
                    mbuf[k * vg + v, :, lanes],
                    (((1,), (1,)), ((), ())),
                    preferred_element_type=jnp.float32,
                )
            return inner

        lax.fori_loop(0, g_total // ht, tile, 0)
        for v in range(vg):
            here = band == me * v_per + k * vg + v
            weight = jnp.sum(jnp.where(here, weights, 0.0), axis=1, keepdims=True)
            acc[...] -= weight * pair[v]
        return carry

    lax.fori_loop(0, nk, group, 0)

    def g_copy(offset):
        return pltpu.make_async_remote_copy(
            src_ref=parts.at[peer(offset)],
            dst_ref=ga_in.at[me],
            send_sem=gsend.at[offset - 1],
            recv_sem=grecv.at[offset - 1],
            device_id={"ga": peer(offset)},
            device_id_type=MESH,
        )

    parts[...] = jnp.zeros_like(parts)
    for j in range(n):
        parts[j, 0:rows, 0:n_state] = acc[j * rows : (j + 1) * rows, :]
    for offset in range(1, n):
        g_copy(offset).start()
    ga_in[me] = parts[me]
    for offset in range(1, n):
        g_copy(offset).wait_recv()
    total = ga_in[0]
    for j in range(1, n):
        total = total + ga_in[j]
    pb_in[my_pb] = total

    def p_copy(offset):
        return pltpu.make_async_remote_copy(
            src_ref=pb_in.at[my_pb],
            dst_ref=pb_in.at[my_pb],
            send_sem=psend.at[offset - 1],
            recv_sem=precv.at[offset - 1],
            device_id={"pb": pb_peer(offset)},
            device_id_type=MESH,
        )

    for offset in range(1, n_pb):
        p_copy(offset).start()
    for offset in range(1, n_pb):
        p_copy(offset).wait_recv()
    result = pb_in[0]
    for j in range(1, n_pb):
        result = result + pb_in[j]
    out[...] = result[0:rows, 0:n_state]

    for offset in range(1, n_pb):
        p_copy(offset).wait_send()
    for offset in range(1, n):
        g_copy(offset).wait_send()
        for k in range(nk):
            m_copy(k, offset).wait_send()
    for source in range(n):
        for chunk in range(nc):

            @pl.when(jnp.logical_and(me > 0, source >= me))
            def _():
                w_copy(source, chunk, -1).wait_send()

            @pl.when(jnp.logical_and(me < n - 1, source <= me))
            def _():
                w_copy(source, chunk, 1).wait_send()


def on_device(n, n_pb, elements, screened, counts, k_minus_q, occupation):
    _, n_band, n_state, g_slab = elements.shape
    g_total = screened.shape[2]
    v_per = n_band // n
    n_cycles = g_slab // NB
    vg = 2 if v_per % 2 == 0 else 1
    nc = min(4, n_cycles)
    wc = n_cycles // nc
    nk = v_per // vg
    rows = n_state // n
    padded = (rows + 7) // 8 * 8
    lanes = (n_state + 127) // 128 * 128
    any_spec = pl.BlockSpec(memory_space=pl.ANY)
    smem = pl.BlockSpec(memory_space=pltpu.SMEM)
    vmem = pl.BlockSpec(memory_space=pltpu.VMEM)
    dma = pltpu.SemaphoreType.DMA
    return pl.pallas_call(
        functools.partial(kernel, n, n_pb, vg, wc),
        out_shape=jax.ShapeDtypeStruct((rows, n_state), jnp.float32),
        in_specs=[any_spec, any_spec, smem, smem, any_spec],
        out_specs=vmem,
        scratch_shapes=[
            pltpu.VMEM((v_per, n_state, g_total), jnp.bfloat16),
            pltpu.VMEM((n_cycles, n, NB, g_total), jnp.bfloat16),
            pltpu.VMEM((n_cycles, NB, g_total), jnp.bfloat16),
            pltpu.VMEM(occupation.shape, jnp.float32),
            pltpu.VMEM((vg, n_state, n_state), jnp.float32),
            pltpu.VMEM((n_state, n_state), jnp.float32),
            pltpu.VMEM((n, padded, lanes), jnp.float32),
            pltpu.VMEM((n, padded, lanes), jnp.float32),
            pltpu.VMEM((n_pb, padded, lanes), jnp.float32),
            dma((3,)),
            dma((2, n, nc)),
            dma((n, nc)),
            dma((n - 1, nk)),
            dma((n - 1, nk)),
            dma((n - 1,)),
            dma((n - 1,)),
            dma((n_pb - 1,)),
            dma((n_pb - 1,)),
        ],
        compiler_params=pltpu.CompilerParams(
            collective_id=0, has_side_effects=True, vmem_limit_bytes=48 * 1024 * 1024
        ),
        cost_estimate=pl.CostEstimate(
            flops=2 * v_per * n_state * g_total * (g_total + n_state),
            bytes_accessed=16 * 1024 * 1024,
            transcendentals=0,
        ),
    )(
        elements.reshape(n, v_per, n_state, g_slab),
        screened.reshape(n_cycles, NB, g_total),
        counts,
        k_minus_q,
        occupation,
    )


def solution(mesh):
    return jax.shard_map(
        functools.partial(on_device, mesh.shape["ga"], mesh.shape["pb"]),
        mesh=mesh,
        in_specs=(P("pb", None, None, "ga"), P("pb", "ga", None), P("pb"), P("pb"), P()),
        out_specs=P("ga", None),
        check_vma=False,
    )
```

time: 629 us -> 299 us (0.48)
  waiting for transfers between devices: 495 us -> 0 us
  Pallas kernels: 0 us -> 294 us
  blocking collectives: 34.2 us -> 0 us
  matrix products: 29.8 us -> 0 us
  local copies, waits for them, and re-layouts: 25 us -> 3.26 us
  other arithmetic: 20.9 us -> 0 us
  between operations: 15.4 us -> 1.32 us
  starting transfers between devices: 7.98 us -> 0 us
    all_gather x1 -> x0, waiting for transfers between devices: 399 us -> none  [on_device(): lax.all_gather(masked[0], 'ga', axis=2, tiled=True)]
    pallas_call x0 -> x1, Pallas kernels: none -> 294 us  [on_device(): pl.pallas_call(functools.partial(kernel, n, n_pb, vg, wc), out_shape=jax....]
    all_to_all x1 -> x0, waiting for transfers between devices: 96.3 us -> none  [on_device(): lax.all_to_all(screened, 'ga', split_axis=2, concat_axis=1, tiled=True)]
    dot_general x3 -> x0, matrix products: 29.8 us -> none  [the longest x1 21.8 us: accumulate(): jnp.dot(segment.reshape(n_band * n_state, piece_rows), screen_q, preferre...]
    psum x1 -> x0, blocking collectives: 22.9 us -> none  [on_device(): result_rows = lax.psum(row_share, 'pb')]
    unnamed x19 -> x4, local copies, waits for them, and re-layouts: 19.4 us -> 3.26 us
    unnamed x2 -> x0, other arithmetic: 14.2 us -> none
    unnamed x1 -> x0, blocking collectives: 11.3 us -> none
  transfers between devices with their start and end apart: 3 -> 0, of which waited for: 3 -> 0; matrix products, arithmetic and copies ran while one was open for 6% -> 0% of each run, Pallas kernels for 0% -> 0%
where the time goes in v1:
time: 299 us
  Pallas kernels  294 us (98%)
  local copies, waits for them, and re-layouts  3.26 us (1%)
    pallas_call x1, Pallas kernels, on_device(): pl.pallas_call(functools.partial(kernel, n, n_pb, vg, wc), out_shape=jax....  294 us

profile of v1, /device:TPU:0, one launch (start us, length us, event | category | flops | bytes accessed | tf_op | source)
XLA Modules:
  0.0 298.8 jit_solution(17017269810539598368)
XLA Ops:
  1.3 1.1 copy.6.occupation
  2.4 0.0 copy-start
  2.4 1.6 copy-done
  4.0 294.3 %shard_map.55 = f32[28,112]{1,0:T(8,128)S(1)} custom-call(bf16[4,16,112,512]{3,2,1,0:T(8,128)(2,1)} %bitcast.3, bf16[16,32,2048]{2,1,0:T(8,128)(2,1)S(1)} %bitcast.2, s32[1]{0:T(128)S(6)} %copy.8.counts, s32[1]{0:T(128)S(6)} %copy.9.k_minus_q, f32[576,64]{1,0:T(8,128)S(1)} %copy.6.occupation), custom_call_target="tpu_custom_call" | custom-call | flops 15854469120 | bytes 16777216 | tf_op jit(solution)/shard_map/pallas_call | solution.py:242
  298.2 0.6 copy.10
Async XLA Ops:
  2.4 1.6 copy-start

commit v2 on v1

--- a/solution.py
+++ b/solution.py
@@ -69,10 +69,18 @@
 
     started = []
 
+    def is_end(offset):
+        return jnp.logical_or(peer(offset) == 0, peer(offset) == n - 1)
+
     def send_next_m():
         if len(started) < nk:
-            for offset in range(n - 1, 0, -1):
-                m_copy(len(started), offset).start()
+            k = len(started)
+            for offset in range(1, n):
+
+                @pl.when(jnp.logical_not(is_end(offset)))
+                def _():
+                    m_copy(k, offset).start()
+
             started.append(0)
 
     own_w.wait()
@@ -127,6 +135,12 @@
             send_next_m()
     while len(started) < nk:
         send_next_m()
+    for k in range(nk):
+        for offset in range(1, n):
+
+            @pl.when(is_end(offset))
+            def _():
+                m_copy(k, offset).start()
 
     own_m.wait()
     own_occ.wait()

time: 299 us -> 304 us (1.017)
  Pallas kernels: 294 us -> 299 us
    pallas_call x1, Pallas kernels: 294 us -> 299 us  [on_device(): pl.pallas_call(functools.partial(kernel, n, n_pb, vg, wc), out_shape=jax....]
where the time goes in v2:
time: 304 us; the launch traced here: 303 us
  Pallas kernels  299 us (98%)
  local copies, waits for them, and re-layouts  3.26 us (1%)
    pallas_call x1, Pallas kernels, on_device(): pl.pallas_call(functools.partial(kernel, n, n_pb, vg, wc), out_shape=jax....  299 us

profile of v2, /device:TPU:0, one launch (start us, length us, event | category | flops | bytes accessed | tf_op | source)
XLA Modules:
  0.0 303.4 jit_solution(616016661475166947)
XLA Ops:
  1.3 1.1 copy.6.occupation
  2.4 0.0 copy-start
  2.4 1.6 copy-done
  4.0 298.8 %shard_map.55 = f32[28,112]{1,0:T(8,128)S(1)} custom-call(bf16[4,16,112,512]{3,2,1,0:T(8,128)(2,1)} %bitcast.3, bf16[16,32,2048]{2,1,0:T(8,128)(2,1)S(1)} %bitcast.2, s32[1]{0:T(128)S(6)} %copy.8.counts, s32[1]{0:T(128)S(6)} %copy.9.k_minus_q, f32[576,64]{1,0:T(8,128)S(1)} %copy.6.occupation), custom_call_target="tpu_custom_call" | custom-call | flops 15854469120 | bytes 16777216 | tf_op jit(solution)/shard_map/pallas_call | solution.py:256
  302.8 0.6 copy.10
Async XLA Ops:
  2.4 1.6 copy-start

commit v3 on v1

--- a/solution.py
+++ b/solution.py
@@ -31,9 +31,8 @@
     def pb_peer(offset):
         return lax.rem(my_pb + offset, n_pb)
 
-    my_lanes = pl.ds(pl.multiple_of(me * g_slab, g_slab), g_slab)
     own_w = pltpu.make_async_copy(screened, wown, local_sem.at[0])
-    own_m = pltpu.make_async_copy(elements.at[me], mbuf.at[:, :, my_lanes], local_sem.at[1])
+    own_m = pltpu.make_async_copy(elements.at[me], mbuf.at[me], local_sem.at[1])
     own_occ = pltpu.make_async_copy(occupation, occ, local_sem.at[2])
     own_w.start()
     own_m.start()
@@ -49,7 +48,7 @@
     def m_copy(k, offset):
         return pltpu.make_async_remote_copy(
             src_ref=elements.at[peer(offset), pl.ds(k * vg, vg)],
-            dst_ref=mbuf.at[pl.ds(k * vg, vg), :, my_lanes],
+            dst_ref=mbuf.at[me, pl.ds(k * vg, vg)],
             send_sem=msend.at[offset - 1, k],
             recv_sem=mrecv.at[offset - 1, k],
             device_id={"ga": peer(offset)},
@@ -133,7 +132,6 @@
     weights = occ[pl.ds(k_minus_q[0], 1), :]
     band = lax.broadcasted_iota(jnp.int32, weights.shape, 1)
     acc[...] = jnp.zeros_like(acc)
-    ht = min(512, g_total)
 
     def group(k, carry):
         for offset in range(1, n):
@@ -141,20 +139,22 @@
         pair[...] = jnp.zeros_like(pair)
 
         def tile(h, inner):
-            lanes = pl.ds(pl.multiple_of(h * ht, ht), ht)
-            left = mbuf[pl.ds(k * vg, vg)].reshape(vg * n_state, g_total)
-            w = wbuf[:, :, :, lanes].reshape(g_total, ht)
+            lanes = pl.ds(pl.multiple_of(h * g_slab, g_slab), g_slab)
+            left = jnp.concatenate(
+                [mbuf[a, pl.ds(k * vg, vg)].reshape(vg * n_state, g_slab) for a in range(n)], axis=1
+            )
+            w = wbuf[:, :, :, lanes].reshape(g_total, g_slab)
             product = jnp.dot(left, w, preferred_element_type=jnp.float32).astype(jnp.bfloat16)
             for v in range(vg):
                 pair[v] += lax.dot_general(
                     product[v * n_state : (v + 1) * n_state],
-                    mbuf[k * vg + v, :, lanes],
+                    mbuf[h, k * vg + v],
                     (((1,), (1,)), ((), ())),
                     preferred_element_type=jnp.float32,
                 )
             return inner
 
-        lax.fori_loop(0, g_total // ht, tile, 0)
+        lax.fori_loop(0, n, tile, 0)
         for v in range(vg):
             here = band == me * v_per + k * vg + v
             weight = jnp.sum(jnp.where(here, weights, 0.0), axis=1, keepdims=True)
@@ -245,7 +245,7 @@
         in_specs=[any_spec, any_spec, smem, smem, any_spec],
         out_specs=vmem,
         scratch_shapes=[
-            pltpu.VMEM((v_per, n_state, g_total), jnp.bfloat16),
+            pltpu.VMEM((n, v_per, n_state, g_slab), jnp.bfloat16),
             pltpu.VMEM((n_cycles, n, NB, g_total), jnp.bfloat16),
             pltpu.VMEM((n_cycles, NB, g_total), jnp.bfloat16),
             pltpu.VMEM(occupation.shape, jnp.float32),

time: 299 us -> 299 us (level)
  no operation moved by 1% of the time
where the time goes in v3:
time: 299 us
  Pallas kernels  294 us (98%)
  local copies, waits for them, and re-layouts  3.26 us (1%)
    pallas_call x1, Pallas kernels, on_device(): pl.pallas_call(functools.partial(kernel, n, n_pb, vg, wc), out_shape=jax....  294 us

profile of v3, /device:TPU:0, one launch (start us, length us, event | category | flops | bytes accessed | tf_op | source)
XLA Modules:
  0.0 298.6 jit_solution(8928832854094288305)
XLA Ops:
  1.3 1.1 copy.6.occupation
  2.4 0.0 copy-start
  2.4 1.6 copy-done
  4.0 294.0 %shard_map.55 = f32[28,112]{1,0:T(8,128)S(1)} custom-call(bf16[4,16,112,512]{3,2,1,0:T(8,128)(2,1)} %bitcast.3, bf16[16,32,2048]{2,1,0:T(8,128)(2,1)S(1)} %bitcast.2, s32[1]{0:T(128)S(6)} %copy.8.counts, s32[1]{0:T(128)S(6)} %copy.9.k_minus_q, f32[576,64]{1,0:T(8,128)S(1)} %copy.6.occupation), custom_call_target="tpu_custom_call" | custom-call | flops 15854469120 | bytes 16777216 | tf_op jit(solution)/shard_map/pallas_call | solution.py:242
  298.0 0.6 copy.10
Async XLA Ops:
  2.4 1.6 copy-start

commit v4 on v3

--- a/solution.py
+++ b/solution.py
@@ -32,7 +32,7 @@
         return lax.rem(my_pb + offset, n_pb)
 
     own_w = pltpu.make_async_copy(screened, wown, local_sem.at[0])
-    own_m = pltpu.make_async_copy(elements.at[me], mbuf.at[me], local_sem.at[1])
+    own_m = pltpu.make_async_copy(elements.at[me], mbuf.at[me, me], local_sem.at[1])
     own_occ = pltpu.make_async_copy(occupation, occ, local_sem.at[2])
     own_w.start()
     own_m.start()
@@ -45,13 +45,14 @@
         pl.semaphore_signal(barrier, inc=1, device_id={"pb": pb_peer(offset)}, device_id_type=MESH)
     pl.semaphore_wait(barrier, n - 1 + n_pb - 1)
 
-    def m_copy(k, offset):
+    def hop(src, source, target, k, step):
+        here = (source, target, pl.ds(k * vg, vg))
         return pltpu.make_async_remote_copy(
-            src_ref=elements.at[peer(offset), pl.ds(k * vg, vg)],
-            dst_ref=mbuf.at[me, pl.ds(k * vg, vg)],
-            send_sem=msend.at[offset - 1, k],
-            recv_sem=mrecv.at[offset - 1, k],
-            device_id={"ga": peer(offset)},
+            src_ref=mbuf.at[here] if src is None else src.at[target, pl.ds(k * vg, vg)],
+            dst_ref=mbuf.at[here],
+            send_sem=msend.at[source, target, k],
+            recv_sem=mrecv.at[source, target, k],
+            device_id={"ga": lax.rem(me + step + n, n)},
             device_id_type=MESH,
         )
 
@@ -66,14 +67,6 @@
             device_id_type=MESH,
         )
 
-    started = []
-
-    def send_next_m():
-        if len(started) < nk:
-            for offset in range(n - 1, 0, -1):
-                m_copy(len(started), offset).start()
-            started.append(0)
-
     own_w.wait()
     count = counts[0]
     column = lax.broadcasted_iota(jnp.int32, (NB, g_total), 1)
@@ -98,34 +91,67 @@
         def _():
             w_copy(me, chunk, 1).start()
 
-        if chunk == 0:
-            send_next_m()
-
-    for distance in range(1, n):
-        for chunk in range(nc):
-            source = me - distance
-
-            @pl.when(source >= 0)
-            def _():
-                w_copy(source, chunk, 1).wait_recv()
+    def own_elements(i, carry):
+        reach = n - 1 - i // nk
+        k = lax.rem(i, nk)
+
+        @pl.when(me - reach >= 0)
+        def _():
+            hop(elements, me, me - reach, k, -1).start()
+
+        @pl.when(me + reach < n)
+        def _():
+            hop(elements, me, me + reach, k, 1).start()
+
+        return carry
+
+    lax.fori_loop(0, (n - 1) * nk, own_elements, 0)
+
+    def round_of(distance, carry):
+        low = me - distance
+        high = me + distance
+
+        def pass_w(chunk, inner):
+            @pl.when(low >= 0)
+            def _():
+                w_copy(low, chunk, 1).wait_recv()
 
                 @pl.when(me < n - 1)
                 def _():
-                    w_copy(source, chunk, 1).start()
-
-            source_up = me + distance
-
-            @pl.when(source_up < n)
-            def _():
-                w_copy(source_up, chunk, -1).wait_recv()
+                    w_copy(low, chunk, 1).start()
+
+            @pl.when(high < n)
+            def _():
+                w_copy(high, chunk, -1).wait_recv()
 
                 @pl.when(me > 0)
                 def _():
-                    w_copy(source_up, chunk, -1).start()
-
-            send_next_m()
-    while len(started) < nk:
-        send_next_m()
+                    w_copy(high, chunk, -1).start()
+
+            return inner
+
+        lax.fori_loop(0, nc, pass_w, 0)
+
+        def pass_m(i, inner):
+            reach = n - 1 - i // nk
+            k = lax.rem(i, nk)
+
+            @pl.when(jnp.logical_and(low >= 0, me + reach < n))
+            def _():
+                hop(None, low, me + reach, k, 1).wait_recv()
+                hop(None, low, me + reach, k, 1).start()
+
+            @pl.when(jnp.logical_and(high < n, me - reach >= 0))
+            def _():
+                hop(None, high, me - reach, k, -1).wait_recv()
+                hop(None, high, me - reach, k, -1).start()
+
+            return inner
+
+        lax.fori_loop(0, (n - 1) * nk, pass_m, 0)
+        return carry
+
+    lax.fori_loop(1, n, round_of, 0)
 
     own_m.wait()
     own_occ.wait()
@@ -134,21 +160,25 @@
     acc[...] = jnp.zeros_like(acc)
 
     def group(k, carry):
-        for offset in range(1, n):
-            m_copy(k, offset).wait_recv()
+        for source in range(n):
+
+            @pl.when(source != me)
+            def _():
+                hop(None, source, me, k, 1).wait_recv()
+
         pair[...] = jnp.zeros_like(pair)
 
         def tile(h, inner):
             lanes = pl.ds(pl.multiple_of(h * g_slab, g_slab), g_slab)
             left = jnp.concatenate(
-                [mbuf[a, pl.ds(k * vg, vg)].reshape(vg * n_state, g_slab) for a in range(n)], axis=1
+                [mbuf[a, me, pl.ds(k * vg, vg)].reshape(vg * n_state, g_slab) for a in range(n)], axis=1
             )
             w = wbuf[:, :, :, lanes].reshape(g_total, g_slab)
             product = jnp.dot(left, w, preferred_element_type=jnp.float32).astype(jnp.bfloat16)
             for v in range(vg):
                 pair[v] += lax.dot_general(
                     product[v * n_state : (v + 1) * n_state],
-                    mbuf[h, k * vg + v],
+                    mbuf[h, me, k * vg + v],
                     (((1,), (1,)), ((), ())),
                     preferred_element_type=jnp.float32,
                 )
@@ -209,8 +239,27 @@
         p_copy(offset).wait_send()
     for offset in range(1, n):
         g_copy(offset).wait_send()
-        for k in range(nk):
-            m_copy(k, offset).wait_send()
+
+    def sent_elements(i, carry):
+        source = i // (n * nk)
+        target = lax.rem(i // nk, n)
+        k = lax.rem(i, nk)
+
+        @pl.when(jnp.logical_and(source == me, target != me))
+        def _():
+            hop(elements, source, target, k, 1).wait_send()
+
+        passed = jnp.logical_or(
+            jnp.logical_and(source < me, target > me), jnp.logical_and(source > me, target < me)
+        )
+
+        @pl.when(passed)
+        def _():
+            hop(None, source, target, k, 1).wait_send()
+
+        return carry
+
+    lax.fori_loop(0, n * n * nk, sent_elements, 0)
     for source in range(n):
         for chunk in range(nc):
 
@@ -228,7 +277,7 @@
     g_total = screened.shape[2]
     v_per = n_band // n
     n_cycles = g_slab // NB
-    vg = 2 if v_per % 2 == 0 else 1
+    vg = 4 if v_per % 4 == 0 else 1
     nc = min(4, n_cycles)
     wc = n_cycles // nc
     nk = v_per // vg
@@ -245,7 +294,7 @@
         in_specs=[any_spec, any_spec, smem, smem, any_spec],
         out_specs=vmem,
         scratch_shapes=[
-            pltpu.VMEM((n, v_per, n_state, g_slab), jnp.bfloat16),
+            pltpu.VMEM((n, n, v_per, n_state, g_slab), jnp.bfloat16),
             pltpu.VMEM((n_cycles, n, NB, g_total), jnp.bfloat16),
             pltpu.VMEM((n_cycles, NB, g_total), jnp.bfloat16),
             pltpu.VMEM(occupation.shape, jnp.float32),
@@ -257,15 +306,15 @@
             dma((3,)),
             dma((2, n, nc)),
             dma((n, nc)),
-            dma((n - 1, nk)),
-            dma((n - 1, nk)),
+            dma((n, n, nk)),
+            dma((n, n, nk)),
             dma((n - 1,)),
             dma((n - 1,)),
             dma((n_pb - 1,)),
             dma((n_pb - 1,)),
         ],
         compiler_params=pltpu.CompilerParams(
-            collective_id=0, has_side_effects=True, vmem_limit_bytes=48 * 1024 * 1024
+            collective_id=0, has_side_effects=True, vmem_limit_bytes=56 * 1024 * 1024
         ),
         cost_estimate=pl.CostEstimate(
             flops=2 * v_per * n_state * g_total * (g_total + n_state),

time: 299 us -> 280 us (0.936)
  Pallas kernels: 294 us -> 276 us
    pallas_call x1, Pallas kernels: 294 us -> 276 us  [on_device(): pl.pallas_call(functools.partial(kernel, n, n_pb, vg, wc), out_shape=jax....]
where the time goes in v4:
time: 280 us
  Pallas kernels  276 us (99%)
  local copies, waits for them, and re-layouts  3.1 us (1%)
    pallas_call x1, Pallas kernels, on_device(): pl.pallas_call(functools.partial(kernel, n, n_pb, vg, wc), out_shape=jax....  276 us

profile of v4, /device:TPU:0, one launch (start us, length us, event | category | flops | bytes accessed | tf_op | source)
XLA Modules:
  0.0 280.0 jit_solution(14092083779076072535)
XLA Ops:
  1.3 1.8 copy.6.occupation
  3.1 275.6 %shard_map.55 = f32[28,112]{1,0:T(8,128)} custom-call(bf16[4,16,112,512]{3,2,1,0:T(8,128)(2,1)} %bitcast.2, bf16[16,32,2048]{2,1,0:T(8,128)(2,1)} %bitcast.3, s32[1]{0:T(128)S(6)} %copy.8.counts, s32[1]{0:T(128)S(6)} %copy.9.k_minus_q, f32[576,64]{1,0:T(8,128)} %copy.6.occupation), custom_call_target="tpu_custom_call" | custom-call | flops 15854469120 | bytes 16777216 | tf_op jit(solution)/shard_map/pallas_call | solution.py:291
  278.7 1.3 copy.10

commit v5 on v4

--- a/solution.py
+++ b/solution.py
@@ -14,7 +14,7 @@
 def kernel(
     n, n_pb, vg, wc,
     elements, screened, counts, k_minus_q, occupation, out,
-    mbuf, wbuf, wown, occ, pair, acc, parts, ga_in, pb_in,
+    mbuf, wbuf, wown, occ, prod, pair, acc, parts, ga_in, pb_in,
     local_sem, wsend, wrecv, msend, mrecv, gsend, grecv, psend, precv,
 ):
     me = lax.axis_index("ga")
@@ -32,7 +32,7 @@
         return lax.rem(my_pb + offset, n_pb)
 
     own_w = pltpu.make_async_copy(screened, wown, local_sem.at[0])
-    own_m = pltpu.make_async_copy(elements.at[me], mbuf.at[me, me], local_sem.at[1])
+    own_m = pltpu.make_async_copy(elements, mbuf.at[me], local_sem.at[1])
     own_occ = pltpu.make_async_copy(occupation, occ, local_sem.at[2])
     own_w.start()
     own_m.start()
@@ -56,16 +56,39 @@
             device_id_type=MESH,
         )
 
-    def w_copy(source, chunk, step):
+    def lanes_of(h):
+        return pl.ds(pl.multiple_of(h * g_slab, g_slab), g_slab)
+
+    def first_slab(chunk):
+        return chunk * wc * n * NB // g_slab
+
+    def last_slab(chunk):
+        return ((chunk + 1) * wc * n * NB - 1) // g_slab
+
+    def reaches_left(chunk, h, device):
+        return jnp.logical_or(first_slab(chunk) <= device, h <= device)
+
+    def reaches_right(chunk, h, device):
+        return jnp.logical_or(last_slab(chunk) >= device, h >= device)
+
+    def w_copy(source, chunk, h, step):
         side = 0 if step < 0 else 1
+        piece = chunk * n + h
+        here = (pl.ds(chunk * wc, wc), source, slice(None), lanes_of(h))
         return pltpu.make_async_remote_copy(
-            src_ref=wbuf.at[pl.ds(chunk * wc, wc), source],
-            dst_ref=wbuf.at[pl.ds(chunk * wc, wc), source],
-            send_sem=wsend.at[side, source, chunk],
-            recv_sem=wrecv.at[source, chunk],
+            src_ref=wbuf.at[here],
+            dst_ref=wbuf.at[here],
+            send_sem=wsend.at[side, source, piece],
+            recv_sem=wrecv.at[source, piece],
             device_id={"ga": lax.rem(me + step + n, n)},
             device_id_type=MESH,
         )
+
+    def goes_left(chunk, h):
+        return jnp.logical_and(me > 0, reaches_left(chunk, h, me - 1))
+
+    def goes_right(chunk, h):
+        return jnp.logical_and(me < n - 1, reaches_right(chunk, h, me + 1))
 
     own_w.wait()
     count = counts[0]
@@ -83,13 +106,18 @@
 
         lax.fori_loop(chunk * wc, (chunk + 1) * wc, mask_block, 0)
 
-        @pl.when(me > 0)
-        def _():
-            w_copy(me, chunk, -1).start()
-
-        @pl.when(me < n - 1)
-        def _():
-            w_copy(me, chunk, 1).start()
+        def send_own(h, carry):
+            @pl.when(goes_left(chunk, h))
+            def _():
+                w_copy(me, chunk, h, -1).start()
+
+            @pl.when(goes_right(chunk, h))
+            def _():
+                w_copy(me, chunk, h, 1).start()
+
+            return carry
+
+        lax.fori_loop(0, n, send_own, 0)
 
     def own_elements(i, carry):
         reach = n - 1 - i // nk
@@ -106,52 +134,6 @@
         return carry
 
     lax.fori_loop(0, (n - 1) * nk, own_elements, 0)
-
-    def round_of(distance, carry):
-        low = me - distance
-        high = me + distance
-
-        def pass_w(chunk, inner):
-            @pl.when(low >= 0)
-            def _():
-                w_copy(low, chunk, 1).wait_recv()
-
-                @pl.when(me < n - 1)
-                def _():
-                    w_copy(low, chunk, 1).start()
-
-            @pl.when(high < n)
-            def _():
-                w_copy(high, chunk, -1).wait_recv()
-
-                @pl.when(me > 0)
-                def _():
-                    w_copy(high, chunk, -1).start()
-
-            return inner
-
-        lax.fori_loop(0, nc, pass_w, 0)
-
-        def pass_m(i, inner):
-            reach = n - 1 - i // nk
-            k = lax.rem(i, nk)
-
-            @pl.when(jnp.logical_and(low >= 0, me + reach < n))
-            def _():
-                hop(None, low, me + reach, k, 1).wait_recv()
-                hop(None, low, me + reach, k, 1).start()
-
-            @pl.when(jnp.logical_and(high < n, me - reach >= 0))
-            def _():
-                hop(None, high, me - reach, k, -1).wait_recv()
-                hop(None, high, me - reach, k, -1).start()
-
-            return inner
-
-        lax.fori_loop(0, (n - 1) * nk, pass_m, 0)
-        return carry
-
-    lax.fori_loop(1, n, round_of, 0)
 
     own_m.wait()
     own_occ.wait()
@@ -159,39 +141,129 @@
     band = lax.broadcasted_iota(jnp.int32, weights.shape, 1)
     acc[...] = jnp.zeros_like(acc)
 
-    def group(k, carry):
-        for source in range(n):
-
-            @pl.when(source != me)
-            def _():
-                hop(None, source, me, k, 1).wait_recv()
-
+    def w_block(g, h):
+        if n_cycles % n == 0:
+            cycles = n_cycles // n
+            block = wbuf[pl.ds(g * cycles, cycles), :, :, lanes_of(h)]
+        else:
+            per_cycle = n * NB // g_slab
+            start = lax.rem(g, per_cycle) * (g_slab // NB)
+            block = wbuf[g // per_cycle, pl.ds(start, g_slab // NB), :, lanes_of(h)]
+        return block.reshape(g_slab, g_slab)
+
+    def bands(d, k):
         pair[...] = jnp.zeros_like(pair)
 
-        def tile(h, inner):
-            lanes = pl.ds(pl.multiple_of(h * g_slab, g_slab), g_slab)
-            left = jnp.concatenate(
-                [mbuf[a, me, pl.ds(k * vg, vg)].reshape(vg * n_state, g_slab) for a in range(n)], axis=1
-            )
-            w = wbuf[:, :, :, lanes].reshape(g_total, g_slab)
-            product = jnp.dot(left, w, preferred_element_type=jnp.float32).astype(jnp.bfloat16)
-            for v in range(vg):
-                pair[v] += lax.dot_general(
-                    product[v * n_state : (v + 1) * n_state],
-                    mbuf[h, me, k * vg + v],
-                    (((1,), (1,)), ((), ())),
-                    preferred_element_type=jnp.float32,
-                )
-            return inner
-
-        lax.fori_loop(0, n, tile, 0)
+        def column_slab(h, carry):
+            low = jnp.where(d > me, jnp.where(h == me, 0, me), jnp.where(d == me, jnp.where(h < me, me, 0), me))
+            above = jnp.where(h > me, 0, me + 1)
+            middle = jnp.where(h > me, me + 1, n)
+            below = jnp.where(h == me, n, jnp.where(h > me, me + 1, 0))
+            end = jnp.where(d > me, above, jnp.where(d == me, middle, below))
+
+            @pl.when(low < end)
+            def _():
+                prod[...] = jnp.zeros_like(prod)
+
+                def row_slab(g, inner):
+                    left = mbuf[g, d, pl.ds(k * vg, vg)].reshape(vg * n_state, g_slab)
+                    prod[...] += jnp.dot(left, w_block(g, h), preferred_element_type=jnp.float32)
+                    return inner
+
+                lax.fori_loop(low, end, row_slab, 0)
+                for v in range(vg):
+                    exact = prod[v * n_state : (v + 1) * n_state]
+                    high_part = exact.astype(jnp.bfloat16)
+                    low_part = (exact - high_part.astype(jnp.float32)).astype(jnp.bfloat16)
+                    both = lax.dot_general(
+                        jnp.concatenate([high_part, low_part], axis=0),
+                        mbuf[h, d, k * vg + v],
+                        (((1,), (1,)), ((), ())),
+                        preferred_element_type=jnp.float32,
+                    )
+                    pair[v] += both[:n_state] + both[n_state:]
+
+            return carry
+
+        lax.fori_loop(0, n, column_slab, 0)
         for v in range(vg):
-            here = band == me * v_per + k * vg + v
+            here = band == d * v_per + k * vg + v
             weight = jnp.sum(jnp.where(here, weights, 0.0), axis=1, keepdims=True)
             acc[...] -= weight * pair[v]
+
+    last_round = jnp.maximum(me, n - 1 - me)
+
+    def round_of(distance, carry):
+        low = me - distance
+        high = me + distance
+
+        def pass_w(i, inner):
+            chunk = i // n
+            h = lax.rem(i, n)
+
+            @pl.when(jnp.logical_and(low >= 0, reaches_right(chunk, h, me)))
+            def _():
+                w_copy(low, chunk, h, 1).wait_recv()
+
+                @pl.when(goes_right(chunk, h))
+                def _():
+                    w_copy(low, chunk, h, 1).start()
+
+            @pl.when(jnp.logical_and(high < n, reaches_left(chunk, h, me)))
+            def _():
+                w_copy(high, chunk, h, -1).wait_recv()
+
+                @pl.when(goes_left(chunk, h))
+                def _():
+                    w_copy(high, chunk, h, -1).start()
+
+            return inner
+
+        lax.fori_loop(0, nc * n, pass_w, 0)
+
+        def pass_m(i, inner):
+            reach = n - 1 - i // nk
+            k = lax.rem(i, nk)
+
+            @pl.when(jnp.logical_and(low >= 0, me + reach < n))
+            def _():
+                hop(None, low, me + reach, k, 1).wait_recv()
+                hop(None, low, me + reach, k, 1).start()
+
+            @pl.when(jnp.logical_and(high < n, me - reach >= 0))
+            def _():
+                hop(None, high, me - reach, k, -1).wait_recv()
+                hop(None, high, me - reach, k, -1).start()
+
+            @pl.when(jnp.logical_and(reach == 1, distance == last_round))
+            def _():
+                def others(d, most):
+                    @pl.when(d != me)
+                    def _():
+                        bands(d, k)
+
+                    return most
+
+                lax.fori_loop(0, n, others, 0)
+
+            return inner
+
+        lax.fori_loop(0, (n - 1) * nk, pass_m, 0)
         return carry
 
-    lax.fori_loop(0, nk, group, 0)
+    lax.fori_loop(1, n, round_of, 0)
+
+    def own_bands(k, carry):
+        for source in range(n):
+
+            @pl.when(source != me)
+            def _():
+                hop(None, source, me, k, 1).wait_recv()
+
+        bands(me, k)
+        return carry
+
+    lax.fori_loop(0, nk, own_bands, 0)
 
     def g_copy(offset):
         return pltpu.make_async_remote_copy(
@@ -260,16 +332,23 @@
         return carry
 
     lax.fori_loop(0, n * n * nk, sent_elements, 0)
-    for source in range(n):
-        for chunk in range(nc):
-
-            @pl.when(jnp.logical_and(me > 0, source >= me))
-            def _():
-                w_copy(source, chunk, -1).wait_send()
-
-            @pl.when(jnp.logical_and(me < n - 1, source <= me))
-            def _():
-                w_copy(source, chunk, 1).wait_send()
+
+    def sent_pieces(i, carry):
+        source = i // (nc * n)
+        chunk = lax.rem(i // n, nc)
+        h = lax.rem(i, n)
+
+        @pl.when(jnp.logical_and(source >= me, goes_left(chunk, h)))
+        def _():
+            w_copy(source, chunk, h, -1).wait_send()
+
+        @pl.when(jnp.logical_and(source <= me, goes_right(chunk, h)))
+        def _():
+            w_copy(source, chunk, h, 1).wait_send()
+
+        return carry
+
+    lax.fori_loop(0, n * nc * n, sent_pieces, 0)
 
 
 def on_device(n, n_pb, elements, screened, counts, k_minus_q, occupation):
@@ -298,14 +377,15 @@
             pltpu.VMEM((n_cycles, n, NB, g_total), jnp.bfloat16),
             pltpu.VMEM((n_cycles, NB, g_total), jnp.bfloat16),
             pltpu.VMEM(occupation.shape, jnp.float32),
+            pltpu.VMEM((vg * n_state, g_slab), jnp.float32),
             pltpu.VMEM((vg, n_state, n_state), jnp.float32),
             pltpu.VMEM((n_state, n_state), jnp.float32),
             pltpu.VMEM((n, padded, lanes), jnp.float32),
             pltpu.VMEM((n, padded, lanes), jnp.float32),
             pltpu.VMEM((n_pb, padded, lanes), jnp.float32),
             dma((3,)),
-            dma((2, n, nc)),
-            dma((n, nc)),
+            dma((2, n, nc * n)),
+            dma((n, nc * n)),
             dma((n, n, nk)),
             dma((n, n, nk)),
             dma((n - 1,)),

time: 280 us -> 258 us (0.921)
  Pallas kernels: 276 us -> 253 us
    pallas_call x1, Pallas kernels: 276 us -> 253 us  [on_device(): pl.pallas_call(functools.partial(kernel, n, n_pb, vg, wc), out_shape=jax....]
where the time goes in v5:
time: 258 us; the launch traced here: 257 us
  Pallas kernels  253 us (98%)
  local copies, waits for them, and re-layouts  3.1 us (1%)
    pallas_call x1, Pallas kernels, on_device(): pl.pallas_call(functools.partial(kernel, n, n_pb, vg, wc), out_shape=jax....  253 us

profile of v5, /device:TPU:0, one launch (start us, length us, event | category | flops | bytes accessed | tf_op | source)
XLA Modules:
  0.0 257.5 jit_solution(14338331320403031871)
XLA Ops:
  1.3 1.8 copy.6.occupation
  3.1 253.0 %shard_map.55 = f32[28,112]{1,0:T(8,128)} custom-call(bf16[4,16,112,512]{3,2,1,0:T(8,128)(2,1)} %bitcast.2, bf16[16,32,2048]{2,1,0:T(8,128)(2,1)} %bitcast.3, s32[1]{0:T(128)S(6)} %copy.8.counts, s32[1]{0:T(128)S(6)} %copy.9.k_minus_q, f32[576,64]{1,0:T(8,128)} %copy.6.occupation), custom_call_target="tpu_custom_call" | custom-call | flops 15854469120 | bytes 16777216 | tf_op jit(solution)/shard_map/pallas_call | solution.py:370
  256.1 1.3 copy.10

commit v6 on v5

--- a/solution.py
+++ b/solution.py
@@ -14,7 +14,7 @@
 def kernel(
     n, n_pb, vg, wc,
     elements, screened, counts, k_minus_q, occupation, out,
-    mbuf, wbuf, wown, occ, prod, pair, acc, parts, ga_in, pb_in,
+    mbuf, wbuf, wown, occ, weights, prod, pair, acc, parts, ga_in, pb_in,
     local_sem, wsend, wrecv, msend, mrecv, gsend, grecv, psend, precv,
 ):
     me = lax.axis_index("ga")
@@ -24,6 +24,7 @@
     rows = n_state // n
     nk = v_per // vg
     nc = n_cycles // wc
+    group = 2 if nk % 2 == 0 else 1
 
     def peer(offset):
         return lax.rem(me + offset, n)
@@ -72,13 +73,13 @@
         return jnp.logical_or(last_slab(chunk) >= device, h >= device)
 
     def w_copy(source, chunk, h, step):
-        side = 0 if step < 0 else 1
+        slot = source if step < 0 else jnp.where(source == me, n, source)
         piece = chunk * n + h
         here = (pl.ds(chunk * wc, wc), source, slice(None), lanes_of(h))
         return pltpu.make_async_remote_copy(
             src_ref=wbuf.at[here],
             dst_ref=wbuf.at[here],
-            send_sem=wsend.at[side, source, piece],
+            send_sem=wsend.at[slot, piece],
             recv_sem=wrecv.at[source, piece],
             device_id={"ga": lax.rem(me + step + n, n)},
             device_id_type=MESH,
@@ -90,6 +91,24 @@
     def goes_right(chunk, h):
         return jnp.logical_and(me < n - 1, reaches_right(chunk, h, me + 1))
 
+    def send_elements(reach, k):
+        @pl.when(me - reach >= 0)
+        def _():
+            hop(elements, me, me - reach, k, -1).start()
+
+        @pl.when(me + reach < n)
+        def _():
+            hop(elements, me, me + reach, k, 1).start()
+
+    def first_elements(i, carry):
+        send_elements(n - 1 - i, 0)
+        return carry
+
+    def more_elements(i, carry):
+        send_elements(n - 1 - i // (nk - 1), 1 + lax.rem(i, nk - 1))
+        return carry
+
+    lax.fori_loop(0, n - 1, first_elements, 0)
     own_w.wait()
     count = counts[0]
     column = lax.broadcasted_iota(jnp.int32, (NB, g_total), 1)
@@ -119,26 +138,13 @@
 
         lax.fori_loop(0, n, send_own, 0)
 
-    def own_elements(i, carry):
-        reach = n - 1 - i // nk
-        k = lax.rem(i, nk)
-
-        @pl.when(me - reach >= 0)
-        def _():
-            hop(elements, me, me - reach, k, -1).start()
-
-        @pl.when(me + reach < n)
-        def _():
-            hop(elements, me, me + reach, k, 1).start()
-
-        return carry
-
-    lax.fori_loop(0, (n - 1) * nk, own_elements, 0)
+    lax.fori_loop(0, (n - 1) * (nk - 1), more_elements, 0)
 
     own_m.wait()
     own_occ.wait()
-    weights = occ[pl.ds(k_minus_q[0], 1), :]
-    band = lax.broadcasted_iota(jnp.int32, weights.shape, 1)
+    k_points = lax.broadcasted_iota(jnp.int32, occ.shape, 1)
+    chosen = jnp.where(k_points == k_minus_q[0], occ[...], 0.0)
+    weights[...] = jnp.broadcast_to(jnp.sum(chosen, axis=1, keepdims=True), weights.shape)
     acc[...] = jnp.zeros_like(acc)
 
     def w_block(g, h):
@@ -151,7 +157,7 @@
             block = wbuf[g // per_cycle, pl.ds(start, g_slab // NB), :, lanes_of(h)]
         return block.reshape(g_slab, g_slab)
 
-    def bands(d, k):
+    def bands(d, first, size):
         pair[...] = jnp.zeros_like(pair)
 
         def column_slab(h, carry):
@@ -163,21 +169,23 @@
 
             @pl.when(low < end)
             def _():
-                prod[...] = jnp.zeros_like(prod)
+                prod[0 : size * n_state] = jnp.zeros((size * n_state, g_slab), jnp.float32)
 
                 def row_slab(g, inner):
-                    left = mbuf[g, d, pl.ds(k * vg, vg)].reshape(vg * n_state, g_slab)
-                    prod[...] += jnp.dot(left, w_block(g, h), preferred_element_type=jnp.float32)
+                    left = mbuf[g, d, pl.ds(first, size)].reshape(size * n_state, g_slab)
+                    prod[0 : size * n_state] += jnp.dot(
+                        left, w_block(g, h), preferred_element_type=jnp.float32
+                    )
                     return inner
 
                 lax.fori_loop(low, end, row_slab, 0)
-                for v in range(vg):
+                for v in range(size):
                     exact = prod[v * n_state : (v + 1) * n_state]
                     high_part = exact.astype(jnp.bfloat16)
                     low_part = (exact - high_part.astype(jnp.float32)).astype(jnp.bfloat16)
                     both = lax.dot_general(
                         jnp.concatenate([high_part, low_part], axis=0),
-                        mbuf[h, d, k * vg + v],
+                        mbuf[h, d, first + v],
                         (((1,), (1,)), ((), ())),
                         preferred_element_type=jnp.float32,
                     )
@@ -186,9 +194,8 @@
             return carry
 
         lax.fori_loop(0, n, column_slab, 0)
-        for v in range(vg):
-            here = band == d * v_per + k * vg + v
-            weight = jnp.sum(jnp.where(here, weights, 0.0), axis=1, keepdims=True)
+        for v in range(size):
+            weight = weights[pl.ds(d * v_per + first + v, 1), 0:n_state]
             acc[...] -= weight * pair[v]
 
     last_round = jnp.maximum(me, n - 1 - me)
@@ -235,12 +242,14 @@
                 hop(None, high, me - reach, k, -1).wait_recv()
                 hop(None, high, me - reach, k, -1).start()
 
-            @pl.when(jnp.logical_and(reach == 1, distance == last_round))
+            group_ends = lax.rem(k, group) == group - 1
+
+            @pl.when(jnp.logical_and(jnp.logical_and(reach == 1, group_ends), distance == last_round))
             def _():
                 def others(d, most):
                     @pl.when(d != me)
                     def _():
-                        bands(d, k)
+                        bands(d, (k - (group - 1)) * vg, group * vg)
 
                     return most
 
@@ -253,17 +262,23 @@
 
     lax.fori_loop(1, n, round_of, 0)
 
-    def own_bands(k, carry):
+    def arrived(k):
         for source in range(n):
 
             @pl.when(source != me)
             def _():
                 hop(None, source, me, k, 1).wait_recv()
 
-        bands(me, k)
-        return carry
-
-    lax.fori_loop(0, nk, own_bands, 0)
+    def own_group(i, carry):
+        for j in range(group):
+            arrived(i * group + j)
+        bands(me, i * group * vg, group * vg)
+        return carry
+
+    lax.fori_loop(0, nk // group - 1, own_group, 0)
+    for k in range(nk - group, nk):
+        arrived(k)
+        bands(me, k * vg, vg)
 
     def g_copy(offset):
         return pltpu.make_async_remote_copy(
@@ -356,10 +371,11 @@
     g_total = screened.shape[2]
     v_per = n_band // n
     n_cycles = g_slab // NB
-    vg = 4 if v_per % 4 == 0 else 1
+    vg = 2 if v_per % 4 == 0 else 1
     nc = min(4, n_cycles)
     wc = n_cycles // nc
     nk = v_per // vg
+    group = 2 if nk % 2 == 0 else 1
     rows = n_state // n
     padded = (rows + 7) // 8 * 8
     lanes = (n_state + 127) // 128 * 128
@@ -376,15 +392,16 @@
             pltpu.VMEM((n, n, v_per, n_state, g_slab), jnp.bfloat16),
             pltpu.VMEM((n_cycles, n, NB, g_total), jnp.bfloat16),
             pltpu.VMEM((n_cycles, NB, g_total), jnp.bfloat16),
-            pltpu.VMEM(occupation.shape, jnp.float32),
-            pltpu.VMEM((vg * n_state, g_slab), jnp.float32),
-            pltpu.VMEM((vg, n_state, n_state), jnp.float32),
+            pltpu.VMEM(occupation.shape[::-1], jnp.float32),
+            pltpu.VMEM((n_band, lanes), jnp.float32),
+            pltpu.VMEM((group * vg * n_state, g_slab), jnp.float32),
+            pltpu.VMEM((group * vg, n_state, n_state), jnp.float32),
             pltpu.VMEM((n_state, n_state), jnp.float32),
             pltpu.VMEM((n, padded, lanes), jnp.float32),
             pltpu.VMEM((n, padded, lanes), jnp.float32),
             pltpu.VMEM((n_pb, padded, lanes), jnp.float32),
             dma((3,)),
-            dma((2, n, nc * n)),
+            dma((n + 1, nc * n)),
             dma((n, nc * n)),
             dma((n, n, nk)),
             dma((n, n, nk)),
@@ -406,7 +423,7 @@
         screened.reshape(n_cycles, NB, g_total),
         counts,
         k_minus_q,
-        occupation,
+        occupation.T,
     )
 
 

time: 258 us -> 258 us (level)
  Pallas kernels: 253 us -> 256 us
where the time goes in v6:
time: 258 us
  Pallas kernels  256 us (99%)
    pallas_call x1, Pallas kernels, on_device(): pl.pallas_call(functools.partial(kernel, n, n_pb, vg, wc), out_shape=jax....  256 us

profile of v6, /device:TPU:0, one launch (start us, length us, event | category | flops | bytes accessed | tf_op | source)
XLA Modules:
  0.0 258.2 jit_solution(10251180328135396472)
XLA Ops:
  1.3 255.6 %shard_map.55 = f32[28,112]{1,0:T(8,128)} custom-call(bf16[4,16,112,512]{3,2,1,0:T(8,128)(2,1)} %bitcast.3, bf16[16,32,2048]{2,1,0:T(8,128)(2,1)} %bitcast.4, s32[1]{0:T(128)S(6)} %copy.7.counts, s32[1]{0:T(128)S(6)} %copy.8.k_minus_q, f32[64,576]{1,0:T(8,128)} %bitcast.5), custom_call_target="tpu_custom_call" | custom-call | flops 15854469120 | bytes 16777216 | tf_op jit(solution)/shard_map/pallas_call | solution.py:386
  256.9 1.3 copy.9

commit v7 on v6

--- a/solution.py
+++ b/solution.py
@@ -138,8 +138,6 @@
 
         lax.fori_loop(0, n, send_own, 0)
 
-    lax.fori_loop(0, (n - 1) * (nk - 1), more_elements, 0)
-
     own_m.wait()
     own_occ.wait()
     k_points = lax.broadcasted_iota(jnp.int32, occ.shape, 1)
@@ -157,7 +155,9 @@
             block = wbuf[g // per_cycle, pl.ds(start, g_slab // NB), :, lanes_of(h)]
         return block.reshape(g_slab, g_slab)
 
-    def bands(d, first, size):
+    far = jnp.where(2 * me < n, n - 1, 0)
+
+    def bands(d, first, size, part=None):
         pair[...] = jnp.zeros_like(pair)
 
         def column_slab(h, carry):
@@ -166,6 +166,13 @@
             middle = jnp.where(h > me, me + 1, n)
             below = jnp.where(h == me, n, jnp.where(h > me, me + 1, 0))
             end = jnp.where(d > me, above, jnp.where(d == me, middle, below))
+            if part == "near":
+                low = jnp.where(far == 0, jnp.maximum(low, 1), low)
+                end = jnp.where(h == far, 0, jnp.where(far == 0, end, jnp.minimum(end, n - 1)))
+            if part == "far":
+                has_far = jnp.logical_and(low <= far, far < end)
+                low = jnp.where(h == far, low, far)
+                end = jnp.where(h == far, end, jnp.where(has_far, far + 1, 0))
 
             @pl.when(low < end)
             def _():
@@ -198,36 +205,49 @@
             weight = weights[pl.ds(d * v_per + first + v, 1), 0:n_state]
             acc[...] -= weight * pair[v]
 
-    last_round = jnp.maximum(me, n - 1 - me)
+    def w_round(distance, carry):
+        low = me - distance
+        high = me + distance
+
+        def pass_w(i, inner):
+            chunk = i // n
+            h = lax.rem(i, n)
+
+            @pl.when(jnp.logical_and(low >= 0, reaches_right(chunk, h, me)))
+            def _():
+                w_copy(low, chunk, h, 1).wait_recv()
+
+                @pl.when(goes_right(chunk, h))
+                def _():
+                    w_copy(low, chunk, h, 1).start()
+
+            @pl.when(jnp.logical_and(high < n, reaches_left(chunk, h, me)))
+            def _():
+                w_copy(high, chunk, h, -1).wait_recv()
+
+                @pl.when(goes_left(chunk, h))
+                def _():
+                    w_copy(high, chunk, h, -1).start()
+
+            return inner
+
+        lax.fori_loop(0, nc * n, pass_w, 0)
+        return carry
+
+    total_more = (n - 1) * (nk - 1)
+
+    def w_and_elements(distance, carry):
+        share = (total_more + n - 2) // (n - 1)
+        start = (distance - 1) * share
+        lax.fori_loop(start, jnp.minimum(start + share, total_more), more_elements, 0)
+        return w_round(distance, carry)
+
+    lax.fori_loop(1, n, w_and_elements, 0)
 
     def round_of(distance, carry):
         low = me - distance
         high = me + distance
 
-        def pass_w(i, inner):
-            chunk = i // n
-            h = lax.rem(i, n)
-
-            @pl.when(jnp.logical_and(low >= 0, reaches_right(chunk, h, me)))
-            def _():
-                w_copy(low, chunk, h, 1).wait_recv()
-
-                @pl.when(goes_right(chunk, h))
-                def _():
-                    w_copy(low, chunk, h, 1).start()
-
-            @pl.when(jnp.logical_and(high < n, reaches_left(chunk, h, me)))
-            def _():
-                w_copy(high, chunk, h, -1).wait_recv()
-
-                @pl.when(goes_left(chunk, h))
-                def _():
-                    w_copy(high, chunk, h, -1).start()
-
-            return inner
-
-        lax.fori_loop(0, nc * n, pass_w, 0)
-
         def pass_m(i, inner):
             reach = n - 1 - i // nk
             k = lax.rem(i, nk)
@@ -243,18 +263,21 @@
                 hop(None, high, me - reach, k, -1).start()
 
             group_ends = lax.rem(k, group) == group - 1
-
-            @pl.when(jnp.logical_and(jnp.logical_and(reach == 1, group_ends), distance == last_round))
-            def _():
-                def others(d, most):
-                    @pl.when(d != me)
-                    def _():
-                        bands(d, (k - (group - 1)) * vg, group * vg)
-
-                    return most
-
-                lax.fori_loop(0, n, others, 0)
-
+            first = (k - (group - 1)) * vg
+            to_right = jnp.logical_and(me + reach < n, distance == jnp.maximum(me, 1))
+            to_left = jnp.logical_and(me - reach >= 0, distance == jnp.maximum(n - 1 - me, 1))
+
+            def side(j, most):
+                d = jnp.where(j == 0, me + reach, me - reach)
+                wanted = jnp.where(j == 0, to_right, to_left)
+
+                @pl.when(jnp.logical_and(group_ends, wanted))
+                def _():
+                    bands(d, first, group * vg)
+
+                return most
+
+            lax.fori_loop(0, 2, side, 0)
             return inner
 
         lax.fori_loop(0, (n - 1) * nk, pass_m, 0)
@@ -262,23 +285,27 @@
 
     lax.fori_loop(1, n, round_of, 0)
 
-    def arrived(k):
+    def arrived(k, is_far):
         for source in range(n):
 
-            @pl.when(source != me)
+            @pl.when(jnp.logical_and(source != me, (far == source) == is_far))
             def _():
                 hop(None, source, me, k, 1).wait_recv()
 
-    def own_group(i, carry):
+    def near_group(i, carry):
         for j in range(group):
-            arrived(i * group + j)
-        bands(me, i * group * vg, group * vg)
-        return carry
-
-    lax.fori_loop(0, nk // group - 1, own_group, 0)
-    for k in range(nk - group, nk):
-        arrived(k)
-        bands(me, k * vg, vg)
+            arrived(i * group + j, False)
+        bands(me, i * group * vg, group * vg, "near")
+        return carry
+
+    lax.fori_loop(0, nk // group, near_group, 0)
+
+    def far_group(k, carry):
+        arrived(k, True)
+        bands(me, k * vg, vg, "far")
+        return carry
+
+    lax.fori_loop(0, nk, far_group, 0)
 
     def g_copy(offset):
         return pltpu.make_async_remote_copy(

time: 258 us -> 254 us (0.984)
  Pallas kernels: 256 us -> 251 us
    pallas_call x1, Pallas kernels: 256 us -> 251 us  [on_device(): pl.pallas_call(functools.partial(kernel, n, n_pb, vg, wc), out_shape=jax....]
where the time goes in v7:
time: 254 us
  Pallas kernels  251 us (99%)
    pallas_call x1, Pallas kernels, on_device(): pl.pallas_call(functools.partial(kernel, n, n_pb, vg, wc), out_shape=jax....  251 us

profile of v7, /device:TPU:0, one launch (start us, length us, event | category | flops | bytes accessed | tf_op | source)
XLA Modules:
  0.0 253.6 jit_solution(3978918671943319907)
XLA Ops:
  1.3 251.0 %shard_map.55 = f32[28,112]{1,0:T(8,128)} custom-call(bf16[4,16,112,512]{3,2,1,0:T(8,128)(2,1)} %bitcast.3, bf16[16,32,2048]{2,1,0:T(8,128)(2,1)} %bitcast.4, s32[1]{0:T(128)S(6)} %copy.7.counts, s32[1]{0:T(128)S(6)} %copy.8.k_minus_q, f32[64,576]{1,0:T(8,128)} %bitcast.5), custom_call_target="tpu_custom_call" | custom-call | flops 15854469120 | bytes 16777216 | tf_op jit(solution)/shard_map/pallas_call | solution.py:413
  252.3 1.3 copy.9

commit v8 on v7

--- a/solution.py
+++ b/solution.py
@@ -23,6 +23,9 @@
     n_cycles, _, g_total = screened.shape
     rows = n_state // n
     nk = v_per // vg
+    span = 2 * nk
+    half = n // 2
+    base = lax.rem(my_pb, 2) * half
     nc = n_cycles // wc
     group = 2 if nk % 2 == 0 else 1
 
@@ -45,6 +48,12 @@
     for offset in range(1, n_pb):
         pl.semaphore_signal(barrier, inc=1, device_id={"pb": pb_peer(offset)}, device_id_type=MESH)
     pl.semaphore_wait(barrier, n - 1 + n_pb - 1)
+
+    def is_target(device):
+        return jnp.logical_and(device >= base, device < base + half)
+
+    def set_of(device, i):
+        return 2 * (device - base) + i // nk
 
     def hop(src, source, target, k, step):
         here = (source, target, pl.ds(k * vg, vg))
@@ -67,10 +76,14 @@
         return ((chunk + 1) * wc * n * NB - 1) // g_slab
 
     def reaches_left(chunk, h, device):
-        return jnp.logical_or(first_slab(chunk) <= device, h <= device)
+        least = jnp.minimum(first_slab(chunk), h)
+        most = jnp.maximum(first_slab(chunk), h)
+        return jnp.where(jnp.logical_or(base == 0, device >= half), least, most) <= device
 
     def reaches_right(chunk, h, device):
-        return jnp.logical_or(last_slab(chunk) >= device, h >= device)
+        least = jnp.minimum(last_slab(chunk), h)
+        most = jnp.maximum(last_slab(chunk), h)
+        return jnp.where(jnp.logical_and(base == 0, device >= half), least, most) >= device
 
     def w_copy(source, chunk, h, step):
         slot = source if step < 0 else jnp.where(source == me, n, source)
@@ -91,21 +104,23 @@
     def goes_right(chunk, h):
         return jnp.logical_and(me < n - 1, reaches_right(chunk, h, me + 1))
 
-    def send_elements(reach, k):
-        @pl.when(me - reach >= 0)
-        def _():
-            hop(elements, me, me - reach, k, -1).start()
-
-        @pl.when(me + reach < n)
-        def _():
-            hop(elements, me, me + reach, k, 1).start()
+    def send_elements(reach, i):
+        k = lax.rem(i, nk)
+
+        @pl.when(jnp.logical_and(me - reach >= 0, is_target(me - reach)))
+        def _():
+            hop(elements, me, set_of(me - reach, i), k, -1).start()
+
+        @pl.when(jnp.logical_and(me + reach < n, is_target(me + reach)))
+        def _():
+            hop(elements, me, set_of(me + reach, i), k, 1).start()
 
     def first_elements(i, carry):
         send_elements(n - 1 - i, 0)
         return carry
 
     def more_elements(i, carry):
-        send_elements(n - 1 - i // (nk - 1), 1 + lax.rem(i, nk - 1))
+        send_elements(n - 1 - i // (span - 1), 1 + lax.rem(i, span - 1))
         return carry
 
     lax.fori_loop(0, n - 1, first_elements, 0)
@@ -158,14 +173,15 @@
     far = jnp.where(2 * me < n, n - 1, 0)
 
     def bands(d, first, size, part=None):
+        t = base + d // 2
         pair[...] = jnp.zeros_like(pair)
 
         def column_slab(h, carry):
-            low = jnp.where(d > me, jnp.where(h == me, 0, me), jnp.where(d == me, jnp.where(h < me, me, 0), me))
+            low = jnp.where(t > me, jnp.where(h == me, 0, me), jnp.where(t == me, jnp.where(h < me, me, 0), me))
             above = jnp.where(h > me, 0, me + 1)
             middle = jnp.where(h > me, me + 1, n)
             below = jnp.where(h == me, n, jnp.where(h > me, me + 1, 0))
-            end = jnp.where(d > me, above, jnp.where(d == me, middle, below))
+            end = jnp.where(t > me, above, jnp.where(t == me, middle, below))
             if part == "near":
                 low = jnp.where(far == 0, jnp.maximum(low, 1), low)
                 end = jnp.where(h == far, 0, jnp.where(far == 0, end, jnp.minimum(end, n - 1)))
@@ -234,7 +250,7 @@
         lax.fori_loop(0, nc * n, pass_w, 0)
         return carry
 
-    total_more = (n - 1) * (nk - 1)
+    total_more = (n - 1) * (span - 1)
 
     def w_and_elements(distance, carry):
         share = (total_more + n - 2) // (n - 1)
@@ -249,27 +265,34 @@
         high = me + distance
 
         def pass_m(i, inner):
-            reach = n - 1 - i // nk
-            k = lax.rem(i, nk)
-
-            @pl.when(jnp.logical_and(low >= 0, me + reach < n))
-            def _():
-                hop(None, low, me + reach, k, 1).wait_recv()
-                hop(None, low, me + reach, k, 1).start()
-
-            @pl.when(jnp.logical_and(high < n, me - reach >= 0))
-            def _():
-                hop(None, high, me - reach, k, -1).wait_recv()
-                hop(None, high, me - reach, k, -1).start()
+            reach = n - 1 - i // span
+            j = lax.rem(i, span)
+            k = lax.rem(j, nk)
+            right = me + reach
+            left = me - reach
+            right_ok = jnp.logical_and(right < n, is_target(right))
+            left_ok = jnp.logical_and(left >= 0, is_target(left))
+
+            @pl.when(jnp.logical_and(low >= 0, right_ok))
+            def _():
+                hop(None, low, set_of(right, j), k, 1).wait_recv()
+                hop(None, low, set_of(right, j), k, 1).start()
+
+            @pl.when(jnp.logical_and(high < n, left_ok))
+            def _():
+                hop(None, high, set_of(left, j), k, -1).wait_recv()
+                hop(None, high, set_of(left, j), k, -1).start()
 
             group_ends = lax.rem(k, group) == group - 1
             first = (k - (group - 1)) * vg
-            to_right = jnp.logical_and(me + reach < n, distance == jnp.maximum(me, 1))
-            to_left = jnp.logical_and(me - reach >= 0, distance == jnp.maximum(n - 1 - me, 1))
-
-            def side(j, most):
-                d = jnp.where(j == 0, me + reach, me - reach)
-                wanted = jnp.where(j == 0, to_right, to_left)
+            to_right = jnp.logical_and(right_ok, distance == jnp.maximum(me, 1))
+            to_left = jnp.logical_and(left_ok, distance == jnp.maximum(n - 1 - me, 1))
+
+            def side(which, most):
+                d = jnp.where(which == 0, set_of(right, j), set_of(left, j))
+                wanted = jnp.logical_or(
+                    jnp.logical_and(which == 0, to_right), jnp.logical_and(which == 1, to_left)
+                )
 
                 @pl.when(jnp.logical_and(group_ends, wanted))
                 def _():
@@ -280,32 +303,37 @@
             lax.fori_loop(0, 2, side, 0)
             return inner
 
-        lax.fori_loop(0, (n - 1) * nk, pass_m, 0)
+        lax.fori_loop(0, (n - 1) * span, pass_m, 0)
         return carry
 
     lax.fori_loop(1, n, round_of, 0)
 
-    def arrived(k, is_far):
+    def arrived(d, k, is_far):
         for source in range(n):
 
             @pl.when(jnp.logical_and(source != me, (far == source) == is_far))
             def _():
-                hop(None, source, me, k, 1).wait_recv()
+                hop(None, source, d, k, 1).wait_recv()
 
     def near_group(i, carry):
+        d = set_of(me, i * group)
+        k = lax.rem(i * group, nk)
         for j in range(group):
-            arrived(i * group + j, False)
-        bands(me, i * group * vg, group * vg, "near")
-        return carry
-
-    lax.fori_loop(0, nk // group, near_group, 0)
-
-    def far_group(k, carry):
-        arrived(k, True)
-        bands(me, k * vg, vg, "far")
-        return carry
-
-    lax.fori_loop(0, nk, far_group, 0)
+            arrived(d, k + j, False)
+        bands(d, k * vg, group * vg, "near")
+        return carry
+
+    def far_group(i, carry):
+        d = set_of(me, i)
+        k = lax.rem(i, nk)
+        arrived(d, k, True)
+        bands(d, k * vg, vg, "far")
+        return carry
+
+    @pl.when(is_target(me))
+    def _():
+        lax.fori_loop(0, span // group, near_group, 0)
+        lax.fori_loop(0, span, far_group, 0)
 
     def g_copy(offset):
         return pltpu.make_async_remote_copy(
@@ -356,12 +384,13 @@
 
     def sent_elements(i, carry):
         source = i // (n * nk)
-        target = lax.rem(i // nk, n)
+        d = lax.rem(i // nk, n)
+        target = base + d // 2
         k = lax.rem(i, nk)
 
         @pl.when(jnp.logical_and(source == me, target != me))
         def _():
-            hop(elements, source, target, k, 1).wait_send()
+            hop(elements, source, d, k, 1).wait_send()
 
         passed = jnp.logical_or(
             jnp.logical_and(source < me, target > me), jnp.logical_and(source > me, target < me)
@@ -369,7 +398,7 @@
 
         @pl.when(passed)
         def _():
-            hop(None, source, target, k, 1).wait_send()
+            hop(None, source, d, k, 1).wait_send()
 
         return carry
 

time: 254 us -> 272 us (1.071)
  Pallas kernels: 251 us -> 269 us
    pallas_call x1, Pallas kernels: 251 us -> 269 us  [on_device(): pl.pallas_call(functools.partial(kernel, n, n_pb, vg, wc), out_shape=jax....]
where the time goes in v8:
time: 272 us
  Pallas kernels  269 us (99%)
    pallas_call x1, Pallas kernels, on_device(): pl.pallas_call(functools.partial(kernel, n, n_pb, vg, wc), out_shape=jax....  269 us

profile of v8, /device:TPU:0, one launch (start us, length us, event | category | flops | bytes accessed | tf_op | source)
XLA Modules:
  0.0 271.5 jit_solution(1054185675929018611)
XLA Ops:
  1.3 268.9 %shard_map.55 = f32[28,112]{1,0:T(8,128)} custom-call(bf16[4,16,112,512]{3,2,1,0:T(8,128)(2,1)} %bitcast.3, bf16[16,32,2048]{2,1,0:T(8,128)(2,1)} %bitcast.4, s32[1]{0:T(128)S(6)} %copy.7.counts, s32[1]{0:T(128)S(6)} %copy.8.k_minus_q, f32[64,576]{1,0:T(8,128)} %bitcast.5), custom_call_target="tpu_custom_call" | custom-call | flops 15854469120 | bytes 16777216 | tf_op jit(solution)/shard_map/pallas_call | solution.py:442
  270.2 1.3 copy.9

commit v9 on v7

--- a/solution.py
+++ b/solution.py
@@ -398,7 +398,7 @@
     g_total = screened.shape[2]
     v_per = n_band // n
     n_cycles = g_slab // NB
-    vg = 2 if v_per % 4 == 0 else 1
+    vg = 4 if v_per % 8 == 0 else 2 if v_per % 4 == 0 else 1
     nc = min(4, n_cycles)
     wc = n_cycles // nc
     nk = v_per // vg

time: 254 us -> 252 us (level)
  no operation moved by 1% of the time
where the time goes in v9:
time: 252 us
  Pallas kernels  249 us (99%)
    pallas_call x1, Pallas kernels, on_device(): pl.pallas_call(functools.partial(kernel, n, n_pb, vg, wc), out_shape=jax....  249 us

profile of v9, /device:TPU:0, one launch (start us, length us, event | category | flops | bytes accessed | tf_op | source)
XLA Modules:
  0.0 251.9 jit_solution(17784377613285620369)
XLA Ops:
  1.3 249.3 %shard_map.55 = f32[28,112]{1,0:T(8,128)} custom-call(bf16[4,16,112,512]{3,2,1,0:T(8,128)(2,1)} %bitcast.3, bf16[16,32,2048]{2,1,0:T(8,128)(2,1)} %bitcast.4, s32[1]{0:T(128)S(6)} %copy.7.counts, s32[1]{0:T(128)S(6)} %copy.8.k_minus_q, f32[64,576]{1,0:T(8,128)} %bitcast.5), custom_call_target="tpu_custom_call" | custom-call | flops 15854469120 | bytes 16777216 | tf_op jit(solution)/shard_map/pallas_call | solution.py:413
  250.6 1.3 copy.9
